TPU v7x, 32 devices: a whole 2x2x4 slice. The times are simulated.
32 devices in a mesh: tm: 8 (over z, y), space: 4 (over x, core).
Axes of the slice: x: 2, y: 2, z: 4, core: 2. Of those that a mesh axis runs over, the one named last changes fastest.
Arguments:
- snapshots: bfloat16 [4096, 3, 4096], P('tm', None, 'space'), may hold values from -6 to 6
- cell_weights: float32 [4096], P('space'), may hold values from 0.25 to 4
- triads: int32 [64, 3], replicated, may hold values from 0 to 127, as said below
- owner_slots: int32 [8, 16], replicated, may hold values from -1 to 63, as said below
Outputs:
- bispectra: float32 [128, 512], P(('tm', 'space'))
Inputs may be any that keep to these rules, and one draw needn't show every extreme that they name: `triads`: every row is (k, l, k + l); all three entries are below 128. `owner_slots`: every triad index stands in exactly one slot of the table; in each row the used slots come first and the others hold -1; some owner fills all 16 slots.
All inputs are finite; a program needn't handle non-finite values.
Results may differ from a plain program's by a relative error of at most 0.0076.
Values may be sent and summed in bfloat16 or wider, within the bound.
A program may use at most 64 MiB of HBM per device.

v0:
```python
import math
import jax
import jax.numpy as jnp
from jax import lax
from jax.sharding import PartitionSpec as P

NB = 16
NT = 256
K = 128


def spectral_table():
    sample = jnp.arange(NT, dtype=jnp.int32)
    freq_bins = jnp.arange(K, dtype=jnp.int32)
    phase_idx = freq_bins[:, None] * sample[None, :] % NT
    angles = 2.0 * math.pi / NT * phase_idx.astype(jnp.float32)
    window = 0.5 - 0.5 * jnp.cos(2.0 * math.pi / NT * sample.astype(jnp.float32))
    norm_scale = math.sqrt(8.0 / (3.0 * NT))
    real_rows = norm_scale * window[None, :] * jnp.cos(angles)
    imag_rows = -norm_scale * window[None, :] * jnp.sin(angles)
    return jnp.stack([real_rows, imag_rows], axis=1).reshape(2 * K, NT).astype(jnp.bfloat16)


def transform(piece):
    snap_total, item_count, cell_count = piece.shape
    blocks = piece.reshape(NB, NT, item_count * cell_count)
    spectra = jnp.einsum(
        "jn,bnc->jbc", spectral_table(), blocks, preferred_element_type=jnp.float32
    )
    return spectra.astype(jnp.bfloat16).reshape(K, 2, NB, item_count, cell_count)


def triad_terms(spectra, weight_rows, triads, triad_index):
    count = triad_index.shape[0]
    lane_total = weight_rows.shape[0]
    triad_freqs = jnp.take(triads, triad_index, axis=0)
    first_spec = (
        jnp.take(spectra, triad_freqs[:, 0], axis=0)
        .reshape(count, 2, NB, lane_total)
        .astype(jnp.float32)
    )
    second_spec = (
        jnp.take(spectra, triad_freqs[:, 1], axis=0)
        .reshape(count, 2, NB, lane_total)
        .astype(jnp.float32)
    )
    third_spec = jnp.take(spectra, triad_freqs[:, 2], axis=0).reshape(count, 2, NB, lane_total)
    prod_real = (
        first_spec[:, 0] * second_spec[:, 0] - first_spec[:, 1] * second_spec[:, 1]
    ) * weight_rows
    prod_imag = (
        first_spec[:, 0] * second_spec[:, 1] + first_spec[:, 1] * second_spec[:, 0]
    ) * weight_rows
    product = jnp.stack([prod_real, prod_imag], axis=1).astype(jnp.bfloat16)
    gram = jnp.einsum("trbc,tsdc->trbsd", product, third_spec, preferred_element_type=jnp.float32)
    bis_real = gram[:, 0, :, 0, :] + gram[:, 1, :, 1, :]
    bis_imag = gram[:, 0, :, 1, :] - gram[:, 1, :, 0, :]
    return jnp.stack([bis_real, bis_imag], axis=1).reshape(count, 2 * NB * NB)


def block_size(amount, quantum):
    return quantum * math.gcd(amount // quantum, max(1, 64 // quantum))


def blocked(index_list, quantum, spectra, weight_rows, triads):
    amount = index_list.shape[0]
    width_blk = block_size(amount, quantum)
    grouped = index_list.reshape(amount // width_blk, width_blk)

    def group_terms(slot_group):
        filled = (slot_group >= 0).astype(jnp.float32)
        return (
            triad_terms(spectra, weight_rows, triads, jnp.maximum(slot_group, 0)) * filled[:, None]
        )

    return lax.map(group_terms, grouped).reshape(amount, 2 * NB * NB)


def shards(snapshots, cell_weights, triads, owner_slots):
    spectra = transform(lax.all_to_all(snapshots, "tm", split_axis=2, concat_axis=0, tiled=True))
    cell_count = spectra.shape[4]
    spectra = spectra.reshape(K, 2 * NB * 3 * cell_count)
    tm_total = lax.axis_size("tm")
    space_total = lax.axis_size("space")
    device_total = tm_total * space_total
    weight_scale = 1.0 / math.sqrt(3.0 * cell_count * device_total)
    local_w = (
        lax.dynamic_slice_in_dim(cell_weights, lax.axis_index("tm") * cell_count, cell_count, 0)
        * weight_scale
    )
    weight_rows = jnp.tile(local_w, 3)
    flat_slots = owner_slots.reshape(-1)
    my_rows = flat_slots.shape[0] // device_total
    return lax.psum_scatter(
        blocked(flat_slots, my_rows, spectra, weight_rows, triads),
        ("tm", "space"),
        scatter_dimension=0,
        tiled=True,
    )


def solution(mesh):
    placed = (P("tm", None, "space"), P("space"), P(), P())
    return jax.shard_map(
        shards, mesh=mesh, in_specs=placed, out_specs=P(("tm", "space"), None), check_vma=False
    )
```

profile of v0, /device:TPU:0, one launch (start us, length us, event | category | flops | bytes accessed | tf_op | source)
XLA Modules:
  0.0 327.5 jit_solution(2348501136595664732)
XLA Ops:
  6.5 7.7 %copy.36 = bf16[512,3,1024]{0,1,2:T(4,128)(2,1)} copy(bf16[512,3,1024]{2,0,1:T(8,128)(2,1)} %param.8) | data formatting | bytes 6291456 | tf_op args[0]
  14.2 7.4 %all-to-all-start = ((bf16[512,3,1024]{0,1,2:T(4,128)(2,1)}), bf16[512,3,1024]{0,1,2:T(4,128)(2,1)}, u32[]{:S(2)}, u32[]{:S(2)}) async-start(bf16[512,3,1024]{0,1,2:T(4,128)(2,1)} %copy.36), calls=%async_computation | async-start | bytes 8388608 | tf_op jit(solution)/shard_map/all_to_all | solution.py:80
  23.5 91.4 %all-to-all-done = bf16[512,3,1024]{0,1,2:T(4,128)(2,1)} async-done(((bf16[512,3,1024]{0,1,2:T(4,128)(2,1)}), bf16[512,3,1024]{0,1,2:T(4,128)(2,1)}, u32[]{:S(2)}, u32[]{:S(2)}) %all-to-all-start) | async-done | bytes 3145760 | tf_op jit(solution)/shard_map/all_to_all | solution.py:80
  114.9 4.5 %copy.54 = bf16[512,3,8,128]{0,2,3,1:T(8,128)(2,1)S(1)} copy(bf16[512,3,8,128]{0,1,3,2:T(4,128)(2,1)} %bitcast) | data formatting | bytes 6291456 | tf_op jit(solution)/shard_map/all_to_all | solution.py:80
  119.4 3.4 %reshape.253 = bf16[16,256,384]{1,0,2:T(8,128)(2,1)} reshape(bf16[8,512,3,128]{1,0,3,2:T(8,128)(2,1)S(1)} %bitcast.74) | data formatting | bytes 6291456 | tf_op jit(solution)/shard_map/reshape | solution.py:26
  122.7 4.2 %fusion.12 = bf16[256,16,384]{2,0,1:T(8,128)(2,1)S(1)} fusion(bf16[256,256,1]{1,0,2:T(8,128)(2,1)S(1)} %reshape.310, bf16[16,256,384]{1,0,2:T(8,128)(2,1)} %reshape.253), kind=kOutput, calls=%fused_computation.46 | convolution fusion | flops 806879232 | bytes 6422528 | tf_op jit(solution)/shard_map/jn,bnc->jbc/dot_general | solution.py:27
  127.0 3.5 %copy.39 = bf16[256,16,384]{2,1,0:T(8,128)(2,1)} copy(bf16[256,16,384]{2,0,1:T(8,128)(2,1)S(1)} %fusion.12) | data formatting | bytes 6291456 | tf_op jit(solution)/shard_map/convert_element_type | solution.py:30
  130.5 4.2 %reshape_reshape.7 = bf16[128,12288]{1,0:T(8,128)(2,1)S(1)} reshape(bf16[256,16,384]{2,1,0:T(8,128)(2,1)} %copy.39) | data formatting | bytes 6291456 | tf_op jit(solution)/shard_map/reshape;reshape | solution.py:82
  134.7 60.4 %while.11 = (s32[]{:T(128)}, f32[2,64,512]{2,1,0:T(8,128)}, s32[2,64]{1,0:T(2,128)S(1)}, s32[64,3]{1,0:T(8,128)S(1)}, bf16[128,12288]{1,0:T(8,128)(2,1)S(1)}, /*index=5*/f32[128]{0:T(128)S(1)}, s32[]{:T(128)}) while((s32[]{:T(128)}, f32[2,64,512]{2,1,0:T(8,128)}, s32[2,64]{1,0:T(2,128)S(1)}, s32[64,3]{1,0:T(8,128)S(1)}, ...), condition=%wide.region_1.3_spmd.clone, body=%wide.region_0.2_spmd.clone.sunk | while | flops 61446336 | bytes 69630632 | solution.py:76
  135.7 2.7 gather_fusion.1
  138.4 1.7 select_convert_fusion.4
  140.0 2.2 copy.61
  142.3 2.7 gather_fusion.2
  145.0 1.7 select_convert_fusion.5
  147.2 1.3 copy-done
  148.5 1.7 multiply_convert_fusion.5
  150.2 2.7 gather_fusion.3
  152.9 1.6 broadcast_select_fusion.5
  155.9 2.9 fusion.30
  163.4 1.6 constant_dynamic-update-slice_fusion.2
  165.9 2.7 gather_fusion.1
  168.6 1.7 select_convert_fusion.4
  170.2 2.2 copy.61
  172.5 2.7 gather_fusion.2
  175.2 1.7 select_convert_fusion.5
  178.7 1.7 multiply_convert_fusion.5
  180.4 2.7 gather_fusion.3
  183.1 1.6 broadcast_select_fusion.5
  186.1 2.9 fusion.30
  193.6 1.6 constant_dynamic-update-slice_fusion.2
  195.1 124.2 %all-reduce.3.cloned.1.call-done = f32[128,512]{1,0:T(8,128)} async-done(((f32[128,512]{1,0:T(8,128)}), f32[128,512]{1,0:T(8,128)}) %all-reduce.3.cloned.1.call-update) | async-done | bytes 262160
  319.4 1.3 constant_dynamic-slice_fusion.1
  (71 shorter events, 17.8 us)
Async XLA Ops:
  14.2 8.4 %copy-start.4 = (s32[64,3]{0,1:T(4,128)S(1)}, s32[64,3]{0,1:T(4,128)}, u32[]{:S(2)}) copy-start(s32[64,3]{0,1:T(4,128)} %param.10) | copy-start | bytes 2308
  14.2 8.5 %copy-start.3 = (s32[8,16]{1,0:T(8,128)S(1)}, s32[8,16]{1,0:T(8,128)}, u32[]{:S(2)}) copy-start(s32[8,16]{1,0:T(8,128)} %param.11) | copy-start | bytes 1540
  14.2 100.7 %all-to-all-start = ((bf16[512,3,1024]{0,1,2:T(4,128)(2,1)}), bf16[512,3,1024]{0,1,2:T(4,128)(2,1)}, u32[]{:S(2)}, u32[]{:S(2)}) async-start(bf16[512,3,1024]{0,1,2:T(4,128)(2,1)} %copy.36), calls=%async_computation | async-start | bytes 8388608 | tf_op jit(solution)/shard_map/all_to_all | solution.py:80
  21.6 297.7 %all-reduce.3.cloned.1.call-start = ((), (), s32[]{:S(2)}) async-start(), calls=%async_computation.1 | async-start | bytes 524288
  146.6 1.9 copy-start
  154.5 1.1 copy-start.1
  154.5 1.4 copy-start.2
  176.8 1.9 copy-start
  184.7 1.1 copy-start.1
  184.8 1.4 copy-start.2
Sparse Core Ops, SparseCore 0:
  195.3 124.0 all-reduce.2
where the time goes:
time: 329 us; the launch traced here: 328 us
  waiting for transfers between devices  216 us (66%)
  local copies, waits for them, and re-layouts  63.2 us (19%)
  other arithmetic  17.4 us (5%)
  between operations  13.5 us (4%)
  matrix products  10.1 us (3%)
  starting transfers between devices  7.45 us (2%)
    unnamed x2, waiting for transfers between devices  124 us
    all_to_all x1, waiting for transfers between devices, shards(): lax.all_to_all(snapshots, 'tm', split_axis=2, concat_axis=0, tiled=True)  91.4 us
    while x18, local copies, waits for them, and re-layouts  10.8 us
    unnamed x7, local copies, waits for them, and re-layouts  9.08 us
    all_to_all x1, starting transfers between devices, shards(): lax.all_to_all(snapshots, 'tm', split_axis=2, concat_axis=0, tiled=True)  7.41 us
  transfers between devices with their start and end apart: 2, of which 2 were waited for; matrix products, arithmetic and copies ran while one was open for 1% of the time, Pallas kernels for 0%

commit v1 on v0

--- a/solution.py
+++ b/solution.py
@@ -7,6 +7,13 @@
 NB = 16
 NT = 256
 K = 128
+
+
+def exchange_blocks(array, axis, split, join):
+    size = lax.axis_size(axis)
+    pieces = jnp.stack(jnp.split(array, size, axis=split), axis=0)
+    pieces = lax.all_to_all(pieces, axis, split_axis=0, concat_axis=0)
+    return jnp.concatenate(pieces, axis=join)
 
 
 def spectral_table():
@@ -77,7 +84,7 @@
 
 
 def shards(snapshots, cell_weights, triads, owner_slots):
-    spectra = transform(lax.all_to_all(snapshots, "tm", split_axis=2, concat_axis=0, tiled=True))
+    spectra = transform(exchange_blocks(snapshots, "tm", 2, 0))
     cell_count = spectra.shape[4]
     spectra = spectra.reshape(K, 2 * NB * 3 * cell_count)
     tm_total = lax.axis_size("tm")

time: 329 us -> 312 us (0.948)
  waiting for transfers between devices: 216 us -> 193 us
  local copies, waits for them, and re-layouts: 63.2 us -> 72.1 us
    all_to_all x1, waiting for transfers between devices: 91.4 us -> 68.8 us  [exchange_blocks(): pieces = lax.all_to_all(pieces, axis, split_axis=0, concat_axis=0)]
    another operation x0 -> x3, local copies, waits for them, and re-layouts: none -> 14.1 us  [the longest x2 12.3 us: transform(): blocks = piece.reshape(NB, NT, item_count * cell_count)]
    unnamed x7 -> x13, local copies, waits for them, and re-layouts: 9.08 us -> 13.9 us
    all_to_all x1 -> x0, local copies, waits for them, and re-layouts: 4.48 us -> none  [shards(): lax.all_to_all(snapshots, 'tm', split_axis=2, concat_axis=0, tiled=True)]
    reshape x1 -> x0, local copies, waits for them, and re-layouts: 3.36 us -> none  [transform(): blocks = piece.reshape(NB, NT, item_count * cell_count)]
where the time goes in v1:
time: 312 us; the launch traced here: 311 us
  waiting for transfers between devices  193 us (62%)
  local copies, waits for them, and re-layouts  72.1 us (23%)
  other arithmetic  17.6 us (6%)
  between operations  13.5 us (4%)
  starting transfers between devices  7.45 us (2%)
  matrix products  6.88 us (2%)
    unnamed x2, waiting for transfers between devices  124 us
    all_to_all x1, waiting for transfers between devices, exchange_blocks(): pieces = lax.all_to_all(pieces, axis, split_axis=0, concat_axis=0)  68.8 us
    unnamed x13, local copies, waits for them, and re-layouts  13.9 us
    another operation x2, local copies, waits for them, and re-layouts, transform(): blocks = piece.reshape(NB, NT, item_count * cell_count)  12.3 us
    while x18, local copies, waits for them, and re-layouts  8.67 us
    all_to_all x1, starting transfers between devices, exchange_blocks(): pieces = lax.all_to_all(pieces, axis, split_axis=0, concat_axis=0)  7.41 us
  transfers between devices with their start and end apart: 2, of which 2 were waited for; matrix products, arithmetic and copies ran while one was open for 1% of the time, Pallas kernels for 0%

profile of v1, /device:TPU:0, one launch (start us, length us, event | category | flops | bytes accessed | tf_op | source)
XLA Modules:
  0.0 310.8 jit_solution(11059580950329876665)
XLA Ops:
  6.5 1.8 bitcast_dynamic-update-slice_fusion.7
  8.3 1.8 bitcast_dynamic-update-slice_fusion.6
  10.1 1.8 bitcast_dynamic-update-slice_fusion.5
  11.9 1.8 bitcast_dynamic-update-slice_fusion.4
  13.7 1.8 bitcast_dynamic-update-slice_fusion.3
  15.4 1.8 bitcast_dynamic-update-slice_fusion.2
  17.2 1.8 bitcast_dynamic-update-slice_fusion.1
  19.0 1.8 bitcast_dynamic-update-slice_fusion
  20.8 7.4 %all-to-all-start = ((bf16[8,512,3,128]{3,1,2,0:T(8,128)(2,1)}), bf16[8,512,3,128]{3,1,2,0:T(8,128)(2,1)S(1)}, u32[]{:S(2)}, u32[]{:S(2)}) async-start(bf16[8,512,3,128]{3,1,2,0:T(8,128)(2,1)} %bitcast_dynamic-update-slice_fusion), calls=%async_computation | async-start | bytes 6291456 | tf_op jit(solution)/shard_map/all_to_all | solution.py:15
  30.1 68.8 %all-to-all-done = bf16[8,512,3,128]{3,1,2,0:T(8,128)(2,1)S(1)} async-done(((bf16[8,512,3,128]{3,1,2,0:T(8,128)(2,1)}), bf16[8,512,3,128]{3,1,2,0:T(8,128)(2,1)S(1)}, u32[]{:S(2)}, u32[]{:S(2)}) %all-to-all-start) | async-done | bytes 3145760 | tf_op jit(solution)/shard_map/all_to_all | solution.py:15
  98.9 4.6 %copy.41 = bf16[8,512,3,128]{3,2,1,0:T(4,128)(2,1)} copy(bf16[8,512,3,128]{3,1,2,0:T(8,128)(2,1)S(1)} %all-to-all-done) | data formatting | bytes 6291456 | tf_op jit(solution)/shard_map/reshape;reshape | solution.py:33
  103.6 7.7 %reshape.307 = bf16[16,256,384]{2,1,0:T(8,128)(2,1)S(1)} reshape(bf16[8,512,3,128]{3,2,1,0:T(4,128)(2,1)} %copy.41) | data formatting | bytes 6291456 | tf_op jit(solution)/shard_map/reshape;reshape | solution.py:33
  112.2 3.5 %copy.36 = bf16[256,16,384]{2,1,0:T(8,128)(2,1)} copy(bf16[256,16,384]{2,0,1:T(8,128)(2,1)S(1)} %convolution_convert_fusion) | data formatting | bytes 6291456 | tf_op jit(solution)/shard_map/convert_element_type | solution.py:37
  115.7 4.2 %reshape_reshape.11 = bf16[128,12288]{1,0:T(8,128)(2,1)S(1)} reshape(bf16[256,16,384]{2,1,0:T(8,128)(2,1)} %copy.36) | data formatting | bytes 6291456 | tf_op jit(solution)/shard_map/reshape;reshape | solution.py:89
  119.9 58.5 %while.11 = (s32[]{:T(128)}, f32[2,64,512]{2,1,0:T(8,128)}, s32[2,64]{1,0:T(2,128)S(1)}, s32[64,3]{1,0:T(8,128)S(1)}, bf16[128,12288]{1,0:T(8,128)(2,1)S(1)}, /*index=5*/f32[128]{0:T(128)S(1)}, s32[]{:T(128)}) while((s32[]{:T(128)}, f32[2,64,512]{2,1,0:T(8,128)}, s32[2,64]{1,0:T(2,128)S(1)}, s32[64,3]{1,0:T(8,128)S(1)}, ...), condition=%wide.region_1.3_spmd.clone, body=%wide.region_0.2_spmd.clone.sunk | while | flops 61446336 | bytes 69630632 | solution.py:83
  120.9 2.7 gather_fusion.1
  123.6 1.7 select_convert_fusion.4
  125.3 2.2 copy.54
  127.5 2.7 gather_fusion.2
  133.8 1.7 multiply_convert_fusion.5
  135.5 2.7 gather_fusion.3
  138.1 1.7 broadcast_select_fusion.5
  140.2 2.9 fusion.26
  150.1 2.7 gather_fusion.1
  152.8 1.7 select_convert_fusion.4
  154.5 2.2 copy.54
  156.7 2.7 gather_fusion.2
  163.0 1.7 multiply_convert_fusion.5
  164.7 2.7 gather_fusion.3
  167.4 1.7 broadcast_select_fusion.5
  169.4 3.0 fusion.26
  178.5 124.2 %all-reduce.3.cloned.1.call-done = f32[128,512]{1,0:T(8,128)} async-done(((f32[128,512]{1,0:T(8,128)}), f32[128,512]{1,0:T(8,128)}) %all-reduce.3.cloned.1.call-update) | async-done | bytes 262160
  (78 shorter events, 25.8 us)
Async XLA Ops:
  20.8 8.4 %copy-start.4 = (s32[64,3]{0,1:T(4,128)S(1)}, s32[64,3]{0,1:T(4,128)}, u32[]{:S(2)}) copy-start(s32[64,3]{0,1:T(4,128)} %param.10) | copy-start | bytes 2308
  20.8 8.5 %copy-start.3 = (s32[8,16]{1,0:T(8,128)S(1)}, s32[8,16]{1,0:T(8,128)}, u32[]{:S(2)}) copy-start(s32[8,16]{1,0:T(8,128)} %param.11) | copy-start | bytes 1540
  20.8 78.1 %all-to-all-start = ((bf16[8,512,3,128]{3,1,2,0:T(8,128)(2,1)}), bf16[8,512,3,128]{3,1,2,0:T(8,128)(2,1)S(1)}, u32[]{:S(2)}, u32[]{:S(2)}) async-start(bf16[8,512,3,128]{3,1,2,0:T(8,128)(2,1)} %bitcast_dynamic-update-slice_fusion), calls=%async_computation | async-start | bytes 6291456 | tf_op jit(solution)/shard_map/all_to_all | solution.py:15
  28.2 274.4 %all-reduce.3.cloned.1.call-start = ((), (), s32[]{:S(2)}) async-start(), calls=%async_computation.1 | async-start | bytes 524288
  131.9 1.9 copy-start
  138.1 2.0 copy-start.1
  138.1 2.0 copy-start.2
  161.1 1.9 copy-start
  167.4 2.0 copy-start.1
  167.4 2.0 copy-start.2
Sparse Core Ops, SparseCore 0:
  178.6 124.0 all-reduce.2
